TPU v7x, 32 devices: a whole 2x2x4 slice. The times are simulated.
32 devices in a mesh: dp: 16 (over z, x, core), mp: 2 (over y).
Axes of the slice: x: 2, y: 2, z: 4, core: 2. Of those that a mesh axis runs over, the one named last changes fastest.
Arguments:
- inputs: bfloat16 [16384, 768], P('dp'), may hold values from -6 to 6
- segment_ids: int32 [16384], P('dp'), may hold values from 0 to 6, as said below
- pad_flags: int32 [16384], P('dp'), may hold values from 0 to 1, as said below
- w_query: bfloat16 [768, 768], P(None, 'mp'), may hold values from -0.3125 to 0.3125
- w_key: bfloat16 [768, 768], P(None, 'mp'), may hold values from -0.3125 to 0.3125
- w_value: bfloat16 [768, 768], P(None, 'mp'), may hold values from -0.21875 to 0.21875
- b_query: float32 [768], P('mp'), may hold values from -3 to 3
- b_value: float32 [768], P('mp'), may hold values from -3 to 3
- w_proj: bfloat16 [768, 768], P('mp'), may hold values from -0.875 to 0.875
- b_proj: float32 [768], replicated, may hold values from -3 to 3
- gain_attn: float32 [768], replicated, may hold values from 0.5 to 1.5
- shift_attn: float32 [768], replicated, may hold values from -2 to 2
- w_up: bfloat16 [768, 3072], P(None, 'mp'), may hold values from -0.21875 to 0.21875
- b_up: float32 [3072], P('mp'), may hold values from -3 to 3
- w_down: bfloat16 [3072, 768], P('mp'), may hold values from -0.109375 to 0.109375
- b_down: float32 [768], replicated, may hold values from -3 to 3
- gain_ffn: float32 [768], replicated, may hold values from 0.5 to 1.5
- shift_ffn: float32 [768], replicated, may hold values from -2 to 2
- cotangent: bfloat16 [16384, 768], P('dp'), may hold values from -6 to 6
Outputs:
- outputs: bfloat16 [16384, 768], P('dp')
- grad_inputs: float32 [16384, 768], P('dp')
- grad_query: float32 [768, 768], P('dp', 'mp')
- grad_key: float32 [768, 768], P('dp', 'mp')
- grad_value: float32 [768, 768], P('dp', 'mp')
- grad_bquery: float32 [768], P('mp')
- grad_bvalue: float32 [768], P('mp')
- grad_proj: float32 [768, 768], P('mp', 'dp')
- grad_bproj: float32 [768], replicated
- grad_gain_attn: float32 [768], replicated
- grad_shift_attn: float32 [768], replicated
- grad_up: float32 [768, 3072], P('dp', 'mp')
- grad_bup: float32 [3072], P('mp')
- grad_down: float32 [3072, 768], P('mp', 'dp')
- grad_bdown: float32 [768], replicated
- grad_gain_ffn: float32 [768], replicated
- grad_shift_ffn: float32 [768], replicated
Inputs may be any that keep to these rules, and one draw needn't show every extreme that they name: `segment_ids`: within each aligned run of 512 tokens (one packed sequence) the ids start at 0 and never fall; the largest, 6, is reached in some sequence of every draw. `pad_flags`: 1 marks padding, which fills the last 1 to 128 tokens of every packed sequence.
All inputs are finite; a program needn't handle non-finite values.
Results may differ from a plain program's by a relative error of at most 0.013.
The roundings to bfloat16 on the way count: a program that leaves them out, or rounds other values in their place, can miss the bound.
Values sent between devices are 32-bit elements; how exact they have to be, the bound alone decides.
No kernel may reach another device: no remote copies, remote signals or barrier semaphores. Data moves between devices by JAX's collectives and lax.ppermute only.
A program may use at most 192 MiB of HBM per device.

v0:
```python
import jax
import jax.numpy as jnp
from jax import lax
from jax.sharding import PartitionSpec as P

HD = 64
LENGTH = 512


norm_eps = 1e-05
masked_value = -1000000000.0


def plain_dot(left_mat, right_mat):
    return jnp.dot(left_mat, right_mat, preferred_element_type=jnp.float32)


def contract_rows(left_mat, right_mat):
    return lax.dot_general(
        left_mat, right_mat, (((0,), (0,)), ((), ())), preferred_element_type=jnp.float32
    )


def contract_cols(left_mat, right_mat):
    return lax.dot_general(
        left_mat, right_mat, (((1,), (1,)), ((), ())), preferred_element_type=jnp.float32
    )


def layer_norm(values, gain_vec, shift_vec):
    average = jnp.mean(values, axis=-1, keepdims=True)
    centered = values - average
    variance = jnp.mean(centered * centered, axis=-1, keepdims=True)
    return centered * lax.rsqrt(variance + norm_eps) * gain_vec + shift_vec


def gelu_exact(values):
    return 0.5 * values * (1.0 + lax.erf(values * 2.0 ** (-0.5)))


def by_sequence(tensor):
    return tensor.reshape((tensor.shape[0] // LENGTH, LENGTH) + tensor.shape[1:])


def head_view(tensor):
    return tensor.reshape(tensor.shape[0], tensor.shape[1] // HD, HD)


def sequence_scores(seq_query, seq_keys, segments, padding):
    raw_scores = jnp.einsum(
        "qhd,khd->hqk",
        head_view(seq_query),
        head_view(seq_keys),
        preferred_element_type=jnp.float32,
    )
    positions = jnp.arange(LENGTH)
    allowed = (segments[:, None] == segments[None, :]) & (
        (padding[None, :] == 0) | (positions[:, None] == positions[None, :])
    )
    return jnp.where(allowed[None], raw_scores * HD ** (-0.5), masked_value)


def project_inputs(inputs, w_query, w_key, w_value, b_query, b_value):
    queries = (plain_dot(inputs, w_query) + b_query).astype(jnp.bfloat16)
    key_rows = plain_dot(inputs, w_key).astype(jnp.bfloat16)
    value_rows = (plain_dot(inputs, w_value) + b_value).astype(jnp.bfloat16)
    return (queries, key_rows, value_rows)


def feed_up(normed, w_up, b_up):
    normed_low = normed.astype(jnp.bfloat16)
    up_value = plain_dot(normed_low, w_up) + b_up
    active = gelu_exact(up_value).astype(jnp.bfloat16)
    return (normed_low, up_value, active)


def attend_forward(queries, key_rows, value_rows, segment_ids, pad_flags):

    def per_sequence(pieces):
        seq_query, seq_keys, seq_values, segments, padding = pieces
        scores = sequence_scores(seq_query, seq_keys, segments, padding)
        highest = jnp.max(scores, axis=-1, keepdims=True)
        shifted_exp = jnp.exp(scores - highest)
        row_total = jnp.sum(shifted_exp, axis=-1, keepdims=True)
        weights = (shifted_exp / row_total).astype(jnp.bfloat16)
        context = jnp.einsum(
            "hqk,khd->qhd", weights, head_view(seq_values), preferred_element_type=jnp.float32
        )
        return (
            context.reshape(LENGTH, -1).astype(jnp.bfloat16),
            (highest + jnp.log(row_total))[..., 0],
        )

    context, log_total = lax.map(
        per_sequence,
        (
            by_sequence(queries),
            by_sequence(key_rows),
            by_sequence(value_rows),
            by_sequence(segment_ids),
            by_sequence(pad_flags),
        ),
    )
    return (context.reshape(queries.shape[0], -1), log_total)


def attend_backward(queries, key_rows, value_rows, log_total, d_context, segment_ids, pad_flags):

    def per_sequence(pieces):
        seq_query, seq_keys, seq_values, seq_total, seq_grad, segments, padding = pieces
        scores = sequence_scores(seq_query, seq_keys, segments, padding)
        probability = jnp.exp(scores - seq_total[..., None])
        weights = probability.astype(jnp.bfloat16)
        grad_context = head_view(seq_grad)
        grad_prob = jnp.einsum(
            "qhd,khd->hqk", grad_context, head_view(seq_values), preferred_element_type=jnp.float32
        )
        inner_sum = jnp.sum(probability * grad_prob, axis=-1, keepdims=True)
        grad_raw = (probability * (grad_prob - inner_sum) * HD ** (-0.5)).astype(jnp.bfloat16)
        grad_query = jnp.einsum(
            "hqk,khd->qhd", grad_raw, head_view(seq_keys), preferred_element_type=jnp.float32
        )
        grad_keys = jnp.einsum(
            "hqk,qhd->khd", grad_raw, head_view(seq_query), preferred_element_type=jnp.float32
        )
        grad_values = jnp.einsum(
            "hqk,qhd->khd", weights, grad_context, preferred_element_type=jnp.float32
        )
        feature_width = seq_query.shape[1]
        return (
            grad_query.reshape(LENGTH, feature_width).astype(jnp.bfloat16),
            grad_keys.reshape(LENGTH, feature_width).astype(jnp.bfloat16),
            grad_values.reshape(LENGTH, feature_width).astype(jnp.bfloat16),
        )

    d_queries, d_keys, d_values = lax.map(
        per_sequence,
        (
            by_sequence(queries),
            by_sequence(key_rows),
            by_sequence(value_rows),
            log_total,
            by_sequence(d_context),
            by_sequence(segment_ids),
            by_sequence(pad_flags),
        ),
    )
    token_count = queries.shape[0]
    return (
        d_queries.reshape(token_count, -1),
        d_keys.reshape(token_count, -1),
        d_values.reshape(token_count, -1),
    )


def column_sum(tensor):
    return jnp.sum(tensor, axis=0, dtype=jnp.float32)


def on_device(
    inputs,
    segment_ids,
    pad_flags,
    w_query,
    w_key,
    w_value,
    b_query,
    b_value,
    w_proj,
    b_proj,
    gain_attn,
    shift_attn,
    w_up,
    b_up,
    w_down,
    b_down,
    gain_ffn,
    shift_ffn,
    cotangent,
):
    residual_in = inputs.astype(jnp.float32)
    queries, key_rows, value_rows = project_inputs(
        inputs, w_query, w_key, w_value, b_query, b_value
    )
    context, log_total = attend_forward(queries, key_rows, value_rows, segment_ids, pad_flags)
    attention = lax.psum(plain_dot(context, w_proj), "mp") + b_proj
    hidden = residual_in + attention
    normed = layer_norm(hidden, gain_attn, shift_attn)
    normed_low, up_value, active = feed_up(normed, w_up, b_up)
    ffn_out = lax.psum(plain_dot(active, w_down), "mp") + b_down
    summed = normed + ffn_out
    outputs = layer_norm(summed, gain_ffn, shift_ffn).astype(jnp.bfloat16)
    pull_second = jax.vjp(layer_norm, summed, gain_ffn, shift_ffn)[1]
    d_summed, grad_gain_ffn, grad_shift_ffn = pull_second(cotangent.astype(jnp.float32))
    inputs, w_query, w_key, w_value, b_query, b_value, w_up, b_up, normed, d_summed = (
        lax.optimization_barrier(
            (inputs, w_query, w_key, w_value, b_query, b_value, w_up, b_up, normed, d_summed)
        )
    )
    normed_low, up_value, active = feed_up(normed, w_up, b_up)
    queries, key_rows, value_rows = project_inputs(
        inputs, w_query, w_key, w_value, b_query, b_value
    )
    context, log_total = attend_forward(queries, key_rows, value_rows, segment_ids, pad_flags)
    d_ffn = d_summed.astype(jnp.bfloat16)
    grad_bdown = column_sum(d_ffn)
    grad_down = contract_rows(active, d_ffn)
    gelu_pull = jax.vjp(gelu_exact, up_value)[1]
    d_up = gelu_pull(contract_cols(d_ffn, w_down))[0].astype(jnp.bfloat16)
    grad_bup = column_sum(d_up)
    grad_up = contract_rows(normed_low, d_up)
    d_normed = d_summed + lax.psum(contract_cols(d_up, w_up), "mp")
    pull_first = jax.vjp(layer_norm, hidden, gain_attn, shift_attn)[1]
    d_hidden, grad_gain_attn, grad_shift_attn = pull_first(d_normed)
    d_attn = d_hidden.astype(jnp.bfloat16)
    grad_bproj = column_sum(d_attn)
    grad_proj = contract_rows(context, d_attn)
    d_context = contract_cols(d_attn, w_proj).astype(jnp.bfloat16)
    d_queries, d_keys, d_values = attend_backward(
        queries, key_rows, value_rows, log_total, d_context, segment_ids, pad_flags
    )
    grad_bquery = column_sum(d_queries)
    grad_bvalue = column_sum(d_values)
    grad_query = contract_rows(inputs, d_queries)
    grad_key = contract_rows(inputs, d_keys)
    grad_value = contract_rows(inputs, d_values)
    back_part = (
        contract_cols(d_queries, w_query)
        + contract_cols(d_keys, w_key)
        + contract_cols(d_values, w_value)
    )
    grad_inputs = d_hidden + lax.psum(back_part, "mp")
    grad_query, grad_key, grad_value, grad_proj, grad_up, grad_down = (
        lax.psum_scatter(grad_query, "dp", scatter_dimension=0, tiled=True),
        lax.psum_scatter(grad_key, "dp", scatter_dimension=0, tiled=True),
        lax.psum_scatter(grad_value, "dp", scatter_dimension=0, tiled=True),
        lax.psum_scatter(grad_proj, "dp", scatter_dimension=1, tiled=True),
        lax.psum_scatter(grad_up, "dp", scatter_dimension=0, tiled=True),
        lax.psum_scatter(grad_down, "dp", scatter_dimension=1, tiled=True),
    )
    (
        grad_bquery,
        grad_bvalue,
        grad_bproj,
        grad_gain_attn,
        grad_shift_attn,
        grad_bup,
        grad_bdown,
        grad_gain_ffn,
        grad_shift_ffn,
    ) = lax.psum(
        (
            grad_bquery,
            grad_bvalue,
            grad_bproj,
            grad_gain_attn,
            grad_shift_attn,
            grad_bup,
            grad_bdown,
            grad_gain_ffn,
            grad_shift_ffn,
        ),
        "dp",
    )
    return (
        outputs,
        grad_inputs,
        grad_query,
        grad_key,
        grad_value,
        grad_bquery,
        grad_bvalue,
        grad_proj,
        grad_bproj,
        grad_gain_attn,
        grad_shift_attn,
        grad_up,
        grad_bup,
        grad_down,
        grad_bdown,
        grad_gain_ffn,
        grad_shift_ffn,
    )


def solution(mesh):
    placed = (
        P("dp", None),
        P("dp"),
        P("dp"),
        P(None, "mp"),
        P(None, "mp"),
        P(None, "mp"),
        P("mp"),
        P("mp"),
        P("mp", None),
        P(),
        P(),
        P(),
        P(None, "mp"),
        P("mp"),
        P("mp", None),
        P(),
        P(),
        P(),
        P("dp", None),
    )
    return jax.shard_map(
        on_device,
        mesh=mesh,
        in_specs=placed,
        out_specs=(
            P("dp", None),
            P("dp", None),
            P("dp", "mp"),
            P("dp", "mp"),
            P("dp", "mp"),
            P("mp"),
            P("mp"),
            P("mp", "dp"),
            P(),
            P(),
            P(),
            P("dp", "mp"),
            P("mp"),
            P("mp", "dp"),
            P(),
            P(),
            P(),
        ),
        check_vma=False,
    )
```

profile of v0, /device:TPU:0, one launch (start us, length us, event | category | flops | bytes accessed | tf_op | source)
XLA Modules:
  0.0 966.6 jit_solution(7216032282210349604)
XLA Ops:
  17.1 30.3 %while.36 = (s32[]{:T(128)}, bf16[2,512,384]{2,1,0:T(8,128)(2,1)}, bf16[2,512,384]{2,1,0:T(8,128)(2,1)}, s32[2,512]{1,0:T(2,128)S(1)}, s32[2,512]{1,0:T(2,128)S(...) while((s32[]{:T(128)}, bf16[2,512,384]{2,1,0:T(8,128)(2,1)}, ...), condition=%wide.region_3.4_spmd, body=%wide.region_0.3_spmd.sunk | while | flops 413336576 | bytes 21005424 | solution.py:94
  21.6 6.1 fusion.200
  36.8 6.1 fusion.200
  51.4 88.6 %all-reduce.6.cloned.1.call-done = f32[1024,768]{1,0:T(8,128)} async-done(((f32[1024,768]{1,0:T(8,128)}), f32[1024,768]{1,0:T(8,128)}) %all-reduce.6.cloned.1.call-update) | async-done | bytes 3145744 | tf_op jit(solution)/shard_map/psum | solution.py:186
  146.6 8.8 fusion.83
  156.0 85.4 %all-reduce.8.cloned.1.call-done = f32[1024,768]{1,0:T(8,128)} async-done(((f32[1024,768]{1,0:T(8,128)}), f32[1024,768]{1,0:T(8,128)}) %all-reduce.8.cloned.1.call-update) | async-done | bytes 3145744 | tf_op jit(solution)/shard_map/psum | solution.py:190
  272.1 6.0 convert_reduce_fusion
  285.3 13.9 %while.37 = (s32[]{:T(128)}, bf16[2,512,384]{2,1,0:T(8,128)(2,1)}, f32[2,6,512]{2,1,0:T(8,128)S(1)}, bf16[2,512,384]{1,2,0:T(8,128)(2,1)S(1)}, s32[2,512]{1,0:T(...) while((s32[]{:T(128)}, bf16[2,512,384]{2,1,0:T(8,128)(2,1)}, ...), condition=%wide.region_18.19_spmd, body=%wide.region_15.18_spmd.sunk | while | flops 422770176 | bytes 25547900 | solution.py:94
  299.2 70.9 %all-reduce.10.cloned.1.call-done = f32[1024,768]{1,0:T(8,128)} async-done(((f32[1024,768]{1,0:T(8,128)}), f32[1024,768]{1,0:T(8,128)}) %all-reduce.10.cloned.1.call-update) | async-done | bytes 3145744 | tf_op jit(solution)/shard_map/psum | solution.py:212
  370.1 6.3 multiply_reduce_fusion.1
  382.2 78.7 %while.38 = (s32[]{:T(128)}, bf16[2,512,384]{1,2,0:T(8,128)(2,1)}, bf16[2,512,384]{2,1,0:T(8,128)(2,1)}, bf16[2,512,384]{1,2,0:T(8,128)(2,1)}, bf16[2,512,384]{1...) while((s32[]{:T(128)}, bf16[2,512,384]{1,2,0:T(8,128)(2,1)}, ...), condition=%wide.region_21.22_spmd, body=%wide.region_19.21_spmd.sunk | while | flops 1049173504 | bytes 56169632 | solution.py:136
  392.5 10.4 %fusion.224 = bf16[6,64,512]{2,1,0:T(8,128)(2,1)S(1)} fusion(bf16[512,6,64]{0,2,1:T(8,128)(2,1)S(1)} %bitcast.170, f32[6,512,512]{1,2,0:T(8,128)} %fusion.222, f32[6,512,512]{1,2,0:T(8,128)} %fusion.219, f32[6,512]{1,0:T(8,128)S(1)} %dynamic-slice_bitcast_fusion.2, pred[512,512]{0,1:T(8,128)(4,1)S(1)} %fusion.220), kind=kOutput, calls=%fused_computation.61.clone.1 | convolution fusion | flops 218828288 | bytes 13643776 | tf_op jit(solution)/shard_map/while/body/eval_jaxpr/hqk,qhd->khd/dot_general | solution.py:123
  402.9 12.3 %fusion.223 = bf16[6,64,512]{2,1,0:T(8,128)(2,1)S(1)} fusion(bf16[512,6,64]{0,2,1:T(8,128)(2,1)S(1)} %bitcast.168, f32[6,512,512]{1,2,0:T(8,128)} %fusion.222, f32[6,512,512]{1,2,0:T(8,128)} %fusion.219, f32[6,512]{1,0:T(8,128)S(1)} %dynamic-slice_bitcast_fusion.2, pred[512,512]{0,1:T(8,128)(4,1)S(1)} %fusion.220), kind=kOutput, calls=%fused_computation.60.clone.1 | convolution fusion | flops 218828288 | bytes 13643776 | tf_op jit(solution)/shard_map/while/body/eval_jaxpr/hqk,khd->qhd/dot_general | solution.py:120
  431.6 10.4 %fusion.224 = bf16[6,64,512]{2,1,0:T(8,128)(2,1)S(1)} fusion(bf16[512,6,64]{0,2,1:T(8,128)(2,1)S(1)} %bitcast.170, f32[6,512,512]{1,2,0:T(8,128)} %fusion.222, f32[6,512,512]{1,2,0:T(8,128)} %fusion.219, f32[6,512]{1,0:T(8,128)S(1)} %dynamic-slice_bitcast_fusion.2, pred[512,512]{0,1:T(8,128)(4,1)S(1)} %fusion.220), kind=kOutput, calls=%fused_computation.61.clone.1 | convolution fusion | flops 218828288 | bytes 13643776 | tf_op jit(solution)/shard_map/while/body/eval_jaxpr/hqk,qhd->khd/dot_general | solution.py:123
  442.0 12.3 %fusion.223 = bf16[6,64,512]{2,1,0:T(8,128)(2,1)S(1)} fusion(bf16[512,6,64]{0,2,1:T(8,128)(2,1)S(1)} %bitcast.168, f32[6,512,512]{1,2,0:T(8,128)} %fusion.222, f32[6,512,512]{1,2,0:T(8,128)} %fusion.219, f32[6,512]{1,0:T(8,128)S(1)} %dynamic-slice_bitcast_fusion.2, pred[512,512]{0,1:T(8,128)(4,1)S(1)} %fusion.220), kind=kOutput, calls=%fused_computation.60.clone.1 | convolution fusion | flops 218828288 | bytes 13643776 | tf_op jit(solution)/shard_map/while/body/eval_jaxpr/hqk,khd->qhd/dot_general | solution.py:120
  484.6 7.5 fusion.78
  492.2 7.6 fusion.85
  501.6 61.4 %all-reduce = (f32[384]{0:T(512)}, f32[384]{0:T(512)}, f32[768]{0:T(1024)}, f32[768]{0:T(1024)}, f32[768]{0:T(1024)}, /*index=5*/f32[1536]{0:T(1024)}, f32[768]{0:T(1024)}, f32[768]{0:T(1024)}, f32[768]{0:T(1024)}) all-reduce(f32[384]{0:T(512)S(1)} %get-tuple-element.330, ...), channel_id=1, replica_groups=mesh['dp'=16,'mp'=2] {'dp'}, use_global_device_ids=true, to_apply=%region_27.28 | all-reduce | flops 6912 | bytes 55296 | tf_op jit(solution)/shard_map/psum | solution.py:251
  568.0 49.1 %reduce-scatter.13.cloned.1.call-done = f32[384,48]{0,1:T(8,128)} async-done(((f32[384,768]{0,1:T(8,128)}), f32[384,48]{0,1:T(8,128)}) %reduce-scatter.13.cloned.1.call-update) | async-done | bytes 73744 | tf_op jit(solution)/shard_map/reduce_scatter | solution.py:237
  617.1 61.2 %reduce-scatter.11.cloned.1.call-done = f32[48,384]{1,0:T(8,128)} async-done(((f32[768,384]{1,0:T(8,128)}), f32[48,384]{1,0:T(8,128)}) %reduce-scatter.11.cloned.1.call-update) | async-done | bytes 73744 | tf_op jit(solution)/shard_map/reduce_scatter | solution.py:236
  678.3 61.2 %reduce-scatter.7.cloned.1.call-done = f32[48,384]{1,0:T(8,128)} async-done(((f32[768,384]{1,0:T(8,128)}), f32[48,384]{1,0:T(8,128)}) %reduce-scatter.7.cloned.1.call-update) | async-done | bytes 73744 | tf_op jit(solution)/shard_map/reduce_scatter | solution.py:234
  739.5 61.3 %reduce-scatter.9.cloned.1.call-done = f32[48,384]{1,0:T(8,128)} async-done(((f32[768,384]{1,0:T(8,128)}), f32[48,384]{1,0:T(8,128)}) %reduce-scatter.9.cloned.1.call-update) | async-done | bytes 73744 | tf_op jit(solution)/shard_map/reduce_scatter | solution.py:235
  800.8 79.1 %reduce-scatter.17.cloned.1.call-done = f32[1536,48]{0,1:T(8,128)} async-done(((f32[1536,768]{0,1:T(8,128)}), f32[1536,48]{0,1:T(8,128)}) %reduce-scatter.17.cloned.1.call-update) | async-done | bytes 294928 | tf_op jit(solution)/shard_map/reduce_scatter | solution.py:239
  879.9 79.4 %reduce-scatter.15.cloned.1.call-done = f32[48,1536]{1,0:T(8,128)} async-done(((f32[768,1536]{1,0:T(8,128)}), f32[48,1536]{1,0:T(8,128)}) %reduce-scatter.15.cloned.1.call-update) | async-done | bytes 294928 | tf_op jit(solution)/shard_map/reduce_scatter | solution.py:238
  (225 shorter events, 159.4 us)
Async XLA Ops:
  7.2 139.4 %copy-start = (bf16[768,1536]{1,0:T(8,128)(2,1)S(1)}, bf16[768,1536]{1,0:T(8,128)(2,1)}, u32[]{:S(2)}) copy-start(bf16[768,1536]{1,0:T(8,128)(2,1)} %param.37) | copy-start | bytes 7077892
  7.2 5.1 copy-start.38
  7.2 5.1 copy-start.18
  7.2 132.7 %all-reduce.6.cloned.1.call-start = ((), (), s32[]{:S(2)}) async-start(), calls=%async_computation.6 | async-start | bytes 6291456 | tf_op jit(solution)/shard_map/psum | solution.py:186
  8.8 3.5 copy-start.12
  47.3 92.6 %copy-start.32 = (f32[768]{0:T(1024)S(1)}, f32[768]{0:T(1024)}, u32[]{:S(2)}) copy-start(f32[768]{0:T(1024)} %param.34) | copy-start | bytes 9220
  51.3 190.1 %all-reduce.8.cloned.1.call-start = ((), (), s32[]{:S(2)}) async-start(), calls=%async_computation.7 | async-start | bytes 6291456 | tf_op jit(solution)/shard_map/psum | solution.py:190
  155.5 86.0 %copy-start.33 = (f32[768]{0:T(1024)S(1)}, f32[768]{0:T(1024)}, u32[]{:S(2)}) copy-start(f32[768]{0:T(1024)} %param.40) | copy-start | bytes 9220
  155.5 214.6 %all-reduce.10.cloned.1.call-start = ((), (), s32[]{:S(2)}) async-start(), calls=%async_computation.8 | async-start | bytes 6291456 | tf_op jit(solution)/shard_map/psum | solution.py:212
  156.0 89.4 %copy-start.24 = (f32[768]{0:T(1024)S(1)}, f32[768]{0:T(1024)}, u32[]{:S(2)}) copy-start(f32[768]{0:T(1024)} %param.41) | copy-start | bytes 9220
  241.4 4.0 copy-start.6
  267.5 4.6 copy-start.7
  267.5 4.6 copy-start.35
  272.1 6.0 copy-start.40
  284.1 278.9 %all-reduce.12.cloned.1.call-start = ((), (), s32[]{:S(2)}) async-start(), calls=%async_computation.9 | async-start | bytes 6291456 | tf_op jit(solution)/shard_map/psum | solution.py:232
  370.1 6.3 copy-start.3
  469.0 148.1 %reduce-scatter.13.cloned.1.call-start = ((), (), s32[]{:S(2)}) async-start(), calls=%async_computation.13 | async-start | bytes 1253376 | tf_op jit(solution)/shard_map/reduce_scatter | solution.py:237
  473.6 204.7 %reduce-scatter.11.cloned.1.call-start = ((), (), s32[]{:S(2)}) async-start(), calls=%async_computation.12 | async-start | bytes 1253376 | tf_op jit(solution)/shard_map/reduce_scatter | solution.py:236
  477.5 262.0 %reduce-scatter.7.cloned.1.call-start = ((), (), s32[]{:S(2)}) async-start(), calls=%async_computation.10 | async-start | bytes 1253376 | tf_op jit(solution)/shard_map/reduce_scatter | solution.py:234
  481.0 3.6 copy-start.37
  481.1 319.7 %reduce-scatter.9.cloned.1.call-start = ((), (), s32[]{:S(2)}) async-start(), calls=%async_computation.11 | async-start | bytes 1253376 | tf_op jit(solution)/shard_map/reduce_scatter | solution.py:235
  484.6 395.3 %reduce-scatter.17.cloned.1.call-start = ((), (), s32[]{:S(2)}) async-start(), calls=%async_computation.15 | async-start | bytes 5013504 | tf_op jit(solution)/shard_map/reduce_scatter | solution.py:239
  492.2 467.1 %reduce-scatter.15.cloned.1.call-start = ((), (), s32[]{:S(2)}) async-start(), calls=%async_computation.14 | async-start | bytes 5013504 | tf_op jit(solution)/shard_map/reduce_scatter | solution.py:238
  501.6 457.7 %copy-start.1 = (bf16[768,1536]{1,0:T(8,128)(2,1)S(1)}, bf16[768,1536]{1,0:T(8,128)(2,1)}, u32[]{:S(2)}) copy-start(bf16[768,1536]{1,0:T(8,128)(2,1)} %param.37) | copy-start | bytes 7077892
  (27 other events, 54.0 us)
Sparse Core Ops, SparseCore 0:
  51.4 88.4 all-reduce.5
  155.6 85.7 all-reduce.7
  284.3 85.7 all-reduce.9
  469.1 85.7 all-reduce.11
  558.9 58.0 reduce-scatter.12
  621.1 57.1 reduce-scatter.10
  682.5 56.9 reduce-scatter.6
  743.7 57.0 reduce-scatter.8
  805.2 74.6 reduce-scatter.16
  884.6 74.5 reduce-scatter.14
where the time goes:
time: 976 us; the launch traced here: 967 us
  waiting for transfers between devices  636 us (65%)
  matrix products  174 us (18%)
  blocking collectives  61.4 us (6%)
  local copies, waits for them, and re-layouts  41.4 us (4%)
  other arithmetic  36.4 us (4%)
  between operations  15.1 us (2%)
    psum x1, waiting for transfers between devices, on_device(): attention = lax.psum(plain_dot(context, w_proj), 'mp') + b_proj  88.6 us
    psum x1, waiting for transfers between devices, on_device(): ffn_out = lax.psum(plain_dot(active, w_down), 'mp') + b_down  85.4 us
    reduce_scatter x1, waiting for transfers between devices, on_device(): lax.psum_scatter(grad_up, 'dp', scatter_dimension=0, tiled=True)  79.4 us
    reduce_scatter x1, waiting for transfers between devices, on_device(): lax.psum_scatter(grad_down, 'dp', scatter_dimension=1, tiled=True)  79.1 us
    psum x1, waiting for transfers between devices, on_device(): d_normed = d_summed + lax.psum(contract_cols(d_up, w_up), 'mp')  70.9 us
    psum x1, blocking collectives, on_device(): lax.psum((grad_bquery, grad_bvalue, grad_bproj, grad_gain_attn, grad_shif...  61.4 us
    reduce_scatter x1, waiting for transfers between devices, on_device(): lax.psum_scatter(grad_key, 'dp', scatter_dimension=0, tiled=True)  61.3 us
    reduce_scatter x1, waiting for transfers between devices, on_device(): lax.psum_scatter(grad_query, 'dp', scatter_dimension=0, tiled=True)  61.2 us
  transfers between devices with their start and end apart: 10, of which 9 were waited for; matrix products, arithmetic and copies ran while one was open for 5% of the time, Pallas kernels for 0%

commit v1 on v0

v1 whole, which is shorter than its diff:
```python
import functools
import math

import jax
import jax.numpy as jnp
from jax import lax
from jax.experimental import pallas as pl
from jax.experimental.pallas import tpu as pltpu
from jax.sharding import PartitionSpec as P

HD = 64
LENGTH = 512
QUERY_CHUNK = 256
UNIT_BLOCK = 512
norm_eps = 1e-05
masked_value = -1000000000.0
BF = jnp.bfloat16
F32 = jnp.float32
VMEM_BYTES = 50 * 1024 * 1024


def nn(a, b):
    return lax.dot_general(a, b, (((1,), (0,)), ((), ())), preferred_element_type=F32)


def nt(a, b):
    return lax.dot_general(a, b, (((1,), (1,)), ((), ())), preferred_element_type=F32)


def call(body, grid, ins, outs, scratch=(), flops=0):
    def spec(shape, block, index):
        if block == "smem":
            return pl.BlockSpec(memory_space=pltpu.SMEM)
        if block is None:
            return pl.BlockSpec(shape, lambda *_: (0,) * len(shape))
        return pl.BlockSpec(block, index)

    moved = sum(a.size * a.dtype.itemsize for a, _, _ in ins)
    moved += sum(math.prod(s) * jnp.dtype(d).itemsize for s, d, _, _ in outs)
    return pl.pallas_call(
        body,
        grid=grid,
        in_specs=[spec(a.shape, b, i) for a, b, i in ins],
        out_specs=[spec(s, b, i) for s, _, b, i in outs],
        out_shape=[jax.ShapeDtypeStruct(s, d) for s, d, _, _ in outs],
        scratch_shapes=list(scratch),
        compiler_params=pltpu.CompilerParams(vmem_limit_bytes=VMEM_BYTES),
        cost_estimate=pl.CostEstimate(flops=flops, bytes_accessed=moved, transcendentals=0),
    )(*[a for a, _, _ in ins])


def mask_bias(segc_ref, segr_ref, padc_ref, bias_ref):
    shape = bias_ref.shape
    key = lax.broadcasted_iota(jnp.int32, shape, 0)
    query = lax.broadcasted_iota(jnp.int32, shape, 1)
    same = segc_ref[...] == segr_ref[...]
    allowed = same & ((padc_ref[...] == 0) | (key == query))
    bias_ref[...] = jnp.where(allowed, 0.0, masked_value)


def attend_forward(
    x_ref, wq_ref, wk_ref, wv_ref, bq_ref, bv_ref, segc_ref, segr_ref, padc_ref,
    q_ref, k_ref, v_ref, ctx_ref, lse_ref, bias_ref,
):
    x = x_ref[...]
    q_ref[...] = ((nn(x, wq_ref[...]) + bq_ref[...]).astype(BF).astype(F32) * HD ** (-0.5)).astype(BF)
    k_ref[...] = nn(x, wk_ref[...]).astype(BF)
    v_ref[...] = (nn(x, wv_ref[...]) + bv_ref[...]).astype(BF)
    mask_bias(segc_ref, segr_ref, padc_ref, bias_ref)
    length = x.shape[0]

    def pair(index, carry):
        cols = pl.ds(pl.multiple_of(index * 128, 128), 128)
        keys = k_ref[:, cols]
        values_t = v_ref[:, cols].T
        lane = lax.broadcasted_iota(jnp.int32, (QUERY_CHUNK, 128), 1)
        for start in range(0, length, QUERY_CHUNK):
            rows = pl.ds(start, QUERY_CHUNK)
            query = q_ref[rows, cols]
            parts = []
            for head in range(2):
                one = jnp.where((lane < HD) == (head == 0), query, jnp.zeros_like(query))
                scores = nt(keys, one) + bias_ref[:, rows]
                highest = jnp.max(scores, axis=0, keepdims=True)
                grown = jnp.exp(scores - highest)
                total = jnp.sum(grown, axis=0, keepdims=True)
                weights = (grown * (1.0 / total)).astype(BF)
                lse_ref[pl.ds(2 * index + head, 1), rows] = highest + jnp.log(total)
                parts.append(nn(values_t[head * HD:(head + 1) * HD], weights))
            ctx_ref[rows, cols] = jnp.concatenate(parts, axis=0).T.astype(BF)
        return carry

    lax.fori_loop(0, q_ref.shape[1] // 128, pair, 0)


def attend_backward(
    q_ref, k_ref, v_ref, lse_ref, dctx_ref, segc_ref, segr_ref, padc_ref,
    dqkv_ref, sums_ref, bias_ref,
):
    mask_bias(segc_ref, segr_ref, padc_ref, bias_ref)
    length, width = q_ref.shape

    def pair(index, carry):
        first = pl.multiple_of(index * 128, 128)
        cols = pl.ds(first, 128)
        keys = k_ref[:, cols]
        values = v_ref[:, cols]
        keys_t = keys.T
        lane = lax.broadcasted_iota(jnp.int32, (QUERY_CHUNK, 128), 1)
        d_keys = [None, None]
        d_values = [None, None]
        for start in range(0, length, QUERY_CHUNK):
            rows = pl.ds(start, QUERY_CHUNK)
            query = q_ref[rows, cols]
            grad = dctx_ref[rows, cols]
            d_query = []
            for head in range(2):
                here = (lane < HD) == (head == 0)
                scores = nt(keys, jnp.where(here, query, jnp.zeros_like(query))) + bias_ref[:, rows]
                prob = jnp.exp(scores - lse_ref[pl.ds(2 * index + head, 1), rows])
                weights = prob.astype(BF)
                d_prob = nt(values, jnp.where(here, grad, jnp.zeros_like(grad)))
                inner = jnp.sum(prob * d_prob, axis=0, keepdims=True)
                raw = (prob * (d_prob - inner)).astype(BF)
                dv = nn(weights, grad)
                dk = nn(raw, query)
                d_values[head] = dv if start == 0 else d_values[head] + dv
                d_keys[head] = dk if start == 0 else d_keys[head] + dk
                d_query.append(nn(keys_t[head * HD:(head + 1) * HD], raw))
            dq = (jnp.concatenate(d_query, axis=0).T * HD ** (-0.5)).astype(BF)
            dqkv_ref[rows, cols] = dq
        full = lax.broadcasted_iota(jnp.int32, (length, 128), 1) < HD
        dqkv_ref[:, pl.ds(pl.multiple_of(width + first, 128), 128)] = jnp.where(
            full, d_keys[0], d_keys[1]
        ).astype(BF)
        dqkv_ref[:, pl.ds(pl.multiple_of(2 * width + first, 128), 128)] = jnp.where(
            full, d_values[0], d_values[1]
        ).astype(BF)
        return carry

    lax.fori_loop(0, width // 128, pair, 0)
    sums_ref[...] = jnp.broadcast_to(
        jnp.sum(dqkv_ref[...].astype(F32), axis=0, keepdims=True), sums_ref.shape
    )


def moments(values):
    average = jnp.mean(values, axis=-1, keepdims=True)
    centered = values - average
    variance = jnp.mean(centered * centered, axis=-1, keepdims=True)
    inverse = lax.rsqrt(variance + norm_eps)
    return centered * inverse, inverse


def norm_backward(upstream, n, inverse, gain):
    scaled = upstream * gain
    return inverse * (
        scaled
        - jnp.mean(scaled, axis=-1, keepdims=True)
        - n * jnp.mean(scaled * n, axis=-1, keepdims=True)
    )


def down_sum(values):
    return jnp.sum(values, axis=0, keepdims=True)


def feed(nlow, wu_ref, bu_ref, wd_ref, act_ref, slope_ref):
    up = nn(nlow, wu_ref[...]) + bu_ref[...]
    cdf = 0.5 * (1.0 + lax.erf(up * 2.0 ** (-0.5)))
    active = (up * cdf).astype(BF)
    act_ref[...] = active
    slope_ref[...] = cdf + up * jnp.exp(-0.5 * up * up) * (1.0 / math.sqrt(2.0 * math.pi))
    return nn(active, wd_ref[...])


def feed_own(
    x_ref, co_ref, cx_ref, wpo_ref, wpx_ref, bp_ref, g_ref, s_ref, bd_ref, wu_ref, bu_ref, wd_ref,
    hid_ref, nlow_ref, acc_ref, act_ref, slope_ref,
):
    @pl.when(pl.program_id(0) == 0)
    def _():
        attn = nn(co_ref[...], wpo_ref[...]) + nn(cx_ref[...], wpx_ref[...]) + bp_ref[...]
        hidden = x_ref[...].astype(F32) + attn
        hid_ref[...] = hidden
        n, _ = moments(hidden)
        normed = n * g_ref[...] + s_ref[...]
        nlow_ref[...] = normed.astype(BF)
        acc_ref[...] = normed + bd_ref[...]

    acc_ref[...] += feed(nlow_ref[...], wu_ref, bu_ref, wd_ref, act_ref, slope_ref)


def feed_other(
    nlow_ref, start_ref, wu_ref, bu_ref, wd_ref, g_ref, s_ref, cot_ref,
    act_ref, slope_ref, out_ref, dsum_ref, dffn_ref, stats_ref, acc_ref,
):
    @pl.when(pl.program_id(0) == 0)
    def _():
        acc_ref[...] = start_ref[...]

    acc_ref[...] += feed(nlow_ref[...], wu_ref, bu_ref, wd_ref, act_ref, slope_ref)

    @pl.when(pl.program_id(0) == pl.num_programs(0) - 1)
    def _():
        n, inverse = moments(acc_ref[...])
        out_ref[...] = (n * g_ref[...] + s_ref[...]).astype(BF).astype(F32)
        cot = cot_ref[...].astype(F32)
        d_summed = norm_backward(cot, n, inverse, g_ref[...])
        d_ffn = d_summed.astype(BF)
        dsum_ref[...] = d_summed
        dffn_ref[...] = d_ffn
        stats_ref[...] = jnp.zeros_like(stats_ref)
        stats_ref[0:1] = down_sum(cot * n)
        stats_ref[1:2] = down_sum(cot)
        stats_ref[2:3] = down_sum(d_ffn.astype(F32))


def feed_backward(
    dffn_ref, so_ref, sx_ref, wdo_ref, wdx_ref, wuo_ref, wux_ref, dsum_ref, hid_ref, g_ref,
    wpo_ref, wpx_ref,
    duo_ref, dux_ref, bup_ref, dhid_ref, dattn_ref, dco_ref, dcx_ref, stats_ref, acc_ref,
):
    @pl.when(pl.program_id(0) == 0)
    def _():
        acc_ref[...] = dsum_ref[...]

    d_ffn = dffn_ref[...]
    bup_ref[...] = jnp.zeros_like(bup_ref)
    total = acc_ref[...]
    for row, slope, wd, wu, out in (
        (0, so_ref, wdo_ref, wuo_ref, duo_ref),
        (1, sx_ref, wdx_ref, wux_ref, dux_ref),
    ):
        d_up = (nt(d_ffn, wd[...]) * slope[...]).astype(BF)
        out[...] = d_up
        bup_ref[row:row + 1] = down_sum(d_up.astype(F32))
        total += nt(d_up, wu[...])
    acc_ref[...] = total

    @pl.when(pl.program_id(0) == pl.num_programs(0) - 1)
    def _():
        d_normed = acc_ref[...]
        n, inverse = moments(hid_ref[...])
        d_hidden = norm_backward(d_normed, n, inverse, g_ref[...])
        d_attn = d_hidden.astype(BF)
        dhid_ref[...] = d_hidden
        dattn_ref[...] = d_attn
        dco_ref[...] = nt(d_attn, wpo_ref[...]).astype(BF)
        dcx_ref[...] = nt(d_attn, wpx_ref[...]).astype(BF)
        stats_ref[...] = jnp.zeros_like(stats_ref)
        stats_ref[0:1] = down_sum(d_normed * n)
        stats_ref[1:2] = down_sum(d_normed)
        stats_ref[2:3] = down_sum(d_attn.astype(F32))


def input_gradient(*refs):
    dhid_ref, dqo_ref, dqx_ref = refs[:3]
    weights, out_ref = refs[3:9], refs[9]
    total = dhid_ref[...]
    width = weights[0].shape[1]
    for half, grads in enumerate((dqo_ref, dqx_ref)):
        for part in range(3):
            total += nt(grads[:, part * width:(part + 1) * width], weights[half * 3 + part][...])
    out_ref[...] = total


def gradient_split(core_ref, left_ref, own_ref, oth_ref, keep_ref, send_ref, left_t):
    @pl.when(pl.program_id(0) == 0)
    def _():
        left_t[...] = left_ref[...].T

    first = core_ref[0] == 0
    rows = keep_ref.shape[3]
    across = keep_ref.shape[2]
    for half, right in enumerate((own_ref, oth_ref)):
        g = nn(left_t[...], right[...])
        for block in range(keep_ref.shape[1] * across):
            at = 2 * block * rows
            even, odd = g[at:at + rows], g[at + rows:at + 2 * rows]
            keep_ref[half, block // across, block % across] = jnp.where(first, even, odd)
            send_ref[half, block // across, block % across] = jnp.where(first, odd, even)


def gradient_plain(left_ref, own_ref, oth_ref, keep_ref, send_ref, left_t):
    @pl.when(pl.program_id(0) == 0)
    def _():
        left_t[...] = left_ref[...].T

    keep_ref[...] = nn(left_t[...], own_ref[...])
    send_ref[...] = nn(left_t[...], oth_ref[...])


def join_pieces(place_ref, mine_ref, theirs_ref, out_ref):
    same = pl.program_id(0) // 4 == place_ref[0]

    @pl.when(same)
    def _():
        out_ref[...] = mine_ref[0].astype(BF)

    @pl.when(jnp.logical_not(same))
    def _():
        out_ref[...] = theirs_ref[0].astype(BF)


def join_rows(place_ref, mine_ref, theirs_ref, out_ref):
    same = pl.program_id(0) == place_ref[0]

    @pl.when(same)
    def _():
        out_ref[...] = mine_ref[...].astype(out_ref.dtype)

    @pl.when(jnp.logical_not(same))
    def _():
        out_ref[...] = theirs_ref[...].astype(out_ref.dtype)


def both_sequences(place, mine, theirs, dtype):
    rows, cols = mine.shape
    return pl.pallas_call(
        join_rows,
        out_shape=jax.ShapeDtypeStruct((2 * rows, cols), dtype),
        grid_spec=pltpu.PrefetchScalarGridSpec(
            num_scalar_prefetch=1,
            grid=(2,),
            in_specs=[pl.BlockSpec((rows, cols), lambda i, p: (0, 0))] * 2,
            out_specs=pl.BlockSpec((rows, cols), lambda i, p: (i, 0)),
        ),
        compiler_params=pltpu.CompilerParams(vmem_limit_bytes=VMEM_BYTES),
        cost_estimate=pl.CostEstimate(flops=0, bytes_accessed=16 * rows * cols, transcendentals=0),
    )(place, mine, theirs)


def pick(array, index, axis):
    return lax.dynamic_index_in_dim(array, index, axis, keepdims=False)


def on_device(
    dp, inputs, segment_ids, pad_flags, w_query, w_key, w_value, b_query, b_value, w_proj, b_proj,
    gain_attn, shift_attn, w_up, b_up, w_down, b_down, gain_ffn, shift_ffn, cotangent,
):
    m = lax.axis_index("mp")
    d = lax.axis_index("dp")
    width = inputs.shape[1]
    half = w_query.shape[1]
    units = w_up.shape[1]
    core, low = d % 2, (d // 2) % 4

    def swap_mp(array):
        return lax.ppermute(array, "mp", [(0, 1), (1, 0)])

    def swap_dp(array, bit):
        return lax.ppermute(array, "dp", [(i, i ^ bit) for i in range(dp)])

    place_m = jnp.reshape(m, (1,)).astype(jnp.int32)
    place_d = jnp.stack([core, low]).astype(jnp.int32)

    def fetch(pieces):
        own = swap_mp(pieces)
        by_x = swap_dp(own, 2)
        by_z = swap_dp(own, 4)
        cut = own.shape[0] // 2
        far_x = swap_dp(by_z[:cut], 2)
        far_z = swap_dp(by_x[cut:], 4)
        mine = jnp.stack([own, by_x, by_z, jnp.concatenate([far_x, far_z], axis=0)])
        theirs = swap_dp(mine, 1)
        _, rows, cols = mine.shape

        def block(at_mine):
            def index(i, p):
                used = (i // 4 == p[0]) == at_mine
                wait = jnp.where((p[0] == 0) == at_mine, 3, 0)
                return (jnp.bitwise_xor(jnp.where(used, i % 4, wait), p[1]), 0, 0)
            return pl.BlockSpec((1, rows, cols), index)

        return pl.pallas_call(
            join_pieces,
            out_shape=jax.ShapeDtypeStruct((8 * rows, cols), BF),
            grid_spec=pltpu.PrefetchScalarGridSpec(
                num_scalar_prefetch=1,
                grid=(8,),
                in_specs=[block(True), block(False)],
                out_specs=pl.BlockSpec((rows, cols), lambda i, p: (i, 0)),
            ),
            compiler_params=pltpu.CompilerParams(vmem_limit_bytes=VMEM_BYTES),
            cost_estimate=pl.CostEstimate(
                flops=0, bytes_accessed=48 * rows * cols, transcendentals=0
            ),
        )(place_d, mine, theirs)

    def eighth(weight):
        rows = weight.shape[0] // 8
        return lax.dynamic_slice_in_dim(weight, (core * 4 + low) * rows, rows, 0).astype(F32)

    qkv_oth = fetch(jnp.concatenate([eighth(w_query), eighth(w_key), eighth(w_value)], axis=1))
    proj_oth = fetch(eighth(w_proj))
    up_oth = fetch(eighth(w_up))
    down_oth = fetch(eighth(w_down))
    bias_oth = swap_mp(jnp.concatenate([b_query, b_value, b_up]).reshape(1, -1))
    bq_oth, bv_oth, bu_oth = (
        bias_oth[:, :half], bias_oth[:, half:2 * half], bias_oth[:, 2 * half:],
    )

    def row(vector):
        return vector.reshape(1, -1)

    own = lambda array: lax.dynamic_slice_in_dim(array, m * LENGTH, LENGTH, 0)
    x, cot = own(inputs), own(cotangent)
    seg, pad = own(segment_ids), own(pad_flags)
    masks = [(seg.reshape(-1, 1), None, None), (row(seg), None, None), (pad.reshape(-1, 1), None, None)]
    square = pltpu.VMEM((LENGTH, LENGTH), F32)
    heads = half // HD
    lanes = (LENGTH, half)

    def attend(weights, bq, bv):
        return call(
            attend_forward, (1,),
            [(x, None, None)] + weights + [(bq, None, None), (bv, None, None)] + masks,
            [(lanes, BF, None, None)] * 4 + [((heads, LENGTH), F32, None, None)],
            [square], flops=6 * LENGTH * width * half + 16 * LENGTH * LENGTH * half,
        )

    def column(array, at):
        return (array, (array.shape[0], half), lambda *_: (0, at))

    own_qkv = [(w_query, None, None), (w_key, None, None), (w_value, None, None)]
    oth_qkv = [column(qkv_oth, at) for at in range(3)]
    q_own, k_own, v_own, ctx_own, lse_own = attend(own_qkv, row(b_query), row(b_value))
    q_oth, k_oth, v_oth, ctx_oth, lse_oth = attend(oth_qkv, bq_oth, bv_oth)

    full = lambda array: (array, None, None)
    steps = units // UNIT_BLOCK
    feed_ins = lambda wu, bu, wd: [
        (wu, (width, UNIT_BLOCK), lambda i: (0, i)),
        (bu, (1, UNIT_BLOCK), lambda i: (0, i)),
        (wd, (UNIT_BLOCK, width), lambda i: (i, 0)),
    ]
    unit_cols = lambda dtype: ((LENGTH, units), dtype, (LENGTH, UNIT_BLOCK), lambda i: (0, i))
    token = lambda dtype: ((LENGTH, width), dtype, None, None)
    stat = ((8, width), F32, None, None)
    hidden, normed_low, partial, act_own, slope_own = call(
        feed_own, (steps,),
        [full(x), full(ctx_own), full(ctx_oth), full(w_proj), full(proj_oth), full(row(b_proj)),
         full(row(gain_attn)), full(row(shift_attn)), full(row(b_down))]
        + feed_ins(w_up, row(b_up), w_down),
        [token(F32), token(BF), token(F32), unit_cols(BF), unit_cols(F32)],
        flops=4 * LENGTH * width * (half + units),
    )
    act_oth, slope_oth, out_own, d_summed, d_ffn, stats_ffn = call(
        feed_other, (steps,),
        [full(normed_low), full(partial)] + feed_ins(up_oth, bu_oth, down_oth)
        + [full(row(gain_ffn)), full(row(shift_ffn)), full(cot)],
        [unit_cols(BF), unit_cols(F32), token(F32), token(F32), token(BF), stat],
        [pltpu.VMEM((LENGTH, width), F32)],
        flops=4 * LENGTH * width * units,
    )
    out_theirs = swap_mp(out_own)

    shards = dp if dp == 16 else 0
    core_arg = jnp.reshape(core, (1,)).astype(jnp.int32)

    def gradient(left, right_own, right_oth, block, start=0, count=None):
        count = count or right_own.shape[1] // block
        cols = count * block
        ins = [
            full(left),
            (right_own, (LENGTH, block), lambda i: (0, i + start)),
            (right_oth, (LENGTH, block), lambda i: (0, i + start)),
        ]
        scratch = [pltpu.VMEM((width, LENGTH), BF)]
        flops = 4 * LENGTH * width * cols
        if not shards:
            plain = ((width, cols), F32, (width, block), lambda i: (0, i))
            return call(gradient_plain, (count,), ins, [plain] * 2, scratch, flops)
        lead = (2, dp // 4, 2, width // dp)
        cut = (lead + (cols,), F32, lead + (block,), lambda i: (0, 0, 0, 0, i))
        return call(
            gradient_split, (count,), [(core_arg, "smem", None)] + ins, [cut] * 2, scratch, flops
        )

    cross, along = (d // 2) % 2, d // 4
    length_z = dp // 4

    def over_y(v):
        return pick(v, 0, 0) + swap_mp(pick(v, 1, 0))

    def over_x(v, axis):
        return pick(v, cross, axis) + swap_dp(pick(v, 1 - cross, axis), 2)

    def over_z(v, axis):
        shard = lambda at: pick(v, jnp.clip(at, 0, length_z - 1), axis)
        right = left = None
        for step in range(1, length_z):
            ahead, behind = shard(along + length_z - step), shard(along - length_z + step)
            if right is not None:
                ahead, behind = ahead + right, behind + left
            right = lax.ppermute(
                ahead, "dp", [(i, i + 4) for i in range(dp) if i // 4 < step]
            )
            left = lax.ppermute(
                behind, "dp", [(i, i - 4) for i in range(dp) if i // 4 >= length_z - step]
            )
        return shard(along) + right + left

    def reduce(keep, send, order):
        if not shards:
            total = keep + swap_mp(send)
            return lax.psum_scatter(total, "dp", scatter_dimension=0, tiled=True)
        v = keep + swap_dp(send, 1)
        names = ["h", "z", "x"]
        for stage in order:
            axis = names.index({"y": "h"}.get(stage, stage))
            if stage == "y":
                v = over_y(v)
            elif stage == "x":
                v = over_x(v, axis)
            else:
                v = over_z(v, axis)
            names.pop(axis)
        return v

    def everyone(vector):
        if not shards:
            return lax.psum(vector, "dp")
        for bit in (1, 2, 4, 8):
            vector = vector + swap_dp(vector, bit)
        return vector

    chunk = units // 2 // 384
    down_parts = [
        reduce(*gradient(d_ffn, act_own, act_oth, 384, at * chunk, chunk), "xzy") for at in range(2)
    ]
    tokens_by_units = lambda array: (array, (LENGTH, UNIT_BLOCK), lambda i: (0, i))
    down_block = lambda array: (array, (UNIT_BLOCK, width), lambda i: (i, 0))
    up_block = lambda array: (array, (width, UNIT_BLOCK), lambda i: (0, i))
    dup_own, dup_oth, sums_up, d_hidden, d_attn, dctx_own, dctx_oth, stats_attn = call(
        feed_backward, (steps,),
        [full(d_ffn), tokens_by_units(slope_own), tokens_by_units(slope_oth), down_block(w_down),
         down_block(down_oth), up_block(w_up), up_block(up_oth), full(d_summed), full(hidden),
         full(row(gain_attn)), full(w_proj), full(proj_oth)],
        [unit_cols(BF), unit_cols(BF), ((8, units), F32, (8, UNIT_BLOCK), lambda i: (0, i)),
         token(F32), token(BF), (lanes, BF, None, None), (lanes, BF, None, None), stat],
        [pltpu.VMEM((LENGTH, width), F32)],
        flops=8 * LENGTH * width * units,
    )
    up_parts = [
        reduce(*gradient(normed_low, dup_own, dup_oth, 384, at * chunk, chunk), "yxz")
        for at in range(2)
    ]
    common = jnp.concatenate([stats_ffn[:3], stats_attn[:3]], axis=0)
    early = jnp.concatenate([common, sums_up[0].reshape(-1, width)], axis=0) + swap_mp(
        jnp.concatenate([common, sums_up[1].reshape(-1, width)], axis=0)
    )
    early = everyone(early)

    proj_part = reduce(*gradient(d_attn, ctx_own, ctx_oth, half), "xzy")

    def attend_back(q, k, v, lse, dctx):
        return call(
            attend_backward, (1,),
            [full(q), full(k), full(v), full(lse), full(dctx)] + masks,
            [((LENGTH, 3 * half), BF, None, None), ((8, 3 * half), F32, None, None)],
            [square], flops=40 * LENGTH * LENGTH * half,
        )

    dqkv_own, sums_own = attend_back(q_own, k_own, v_own, lse_own, dctx_own)
    dqkv_oth, sums_oth = attend_back(q_oth, k_oth, v_oth, lse_oth, dctx_oth)
    (grad_x,) = call(
        input_gradient, (1,),
        [full(d_hidden), full(dqkv_own), full(dqkv_oth)] + own_qkv + oth_qkv,
        [token(F32)], flops=12 * LENGTH * width * half,
    )
    grad_x_theirs = swap_mp(grad_x)
    qkv_part = reduce(*gradient(x, dqkv_own, dqkv_oth, half), "zxy")

    def ends(sums):
        return jnp.concatenate([sums[:1, :half], sums[:1, 2 * half:]], axis=1)

    late = everyone(ends(sums_own) + swap_mp(ends(sums_oth)))

    outputs = both_sequences(place_m, out_own, out_theirs, BF)
    grad_inputs = both_sequences(place_m, grad_x, grad_x_theirs, F32)
    grad_up = jnp.concatenate(up_parts, axis=1)
    grad_down = jnp.concatenate(down_parts, axis=1).T
    return (
        outputs,
        grad_inputs,
        qkv_part[:, :half],
        qkv_part[:, half:2 * half],
        qkv_part[:, 2 * half:],
        late[0, :half],
        late[0, half:],
        proj_part.T,
        early[5],
        early[3],
        early[4],
        grad_up,
        early[6:].reshape(-1),
        grad_down,
        early[2],
        early[0],
        early[1],
    )


def solution(mesh):
    placed = (
        P("dp", None), P("dp"), P("dp"), P(None, "mp"), P(None, "mp"), P(None, "mp"), P("mp"),
        P("mp"), P("mp", None), P(), P(), P(), P(None, "mp"), P("mp"), P("mp", None), P(), P(), P(),
        P("dp", None),
    )
    return jax.shard_map(
        functools.partial(on_device, mesh.shape["dp"]),
        mesh=mesh,
        in_specs=placed,
        out_specs=(
            P("dp", None), P("dp", None), P("dp", "mp"), P("dp", "mp"), P("dp", "mp"), P("mp"),
            P("mp"), P("mp", "dp"), P(), P(), P(), P("dp", "mp"), P("mp"), P("mp", "dp"), P(), P(),
            P(),
        ),
        check_vma=False,
    )
```

time: 976 us -> 553 us (0.57)
  waiting for transfers between devices: 636 us -> 180 us
  matrix products: 174 us -> 0 us
  starting transfers between devices: 1.05 us -> 172 us
  Pallas kernels: 0 us -> 118 us
  blocking collectives: 61.4 us -> 0 us
  between operations: 15.1 us -> 2.64 us
    reduce_scatter x6 -> x0, waiting for transfers between devices: 391 us -> none  [the longest x1 79.4 us: on_device(): lax.psum_scatter(grad_up, 'dp', scatter_dimension=0, tiled=True)]
    psum x4 -> x0, waiting for transfers between devices: 245 us -> none  [the longest x1 88.6 us: on_device(): attention = lax.psum(plain_dot(context, w_proj), 'mp') + b_proj]
    ppermute x0 -> x91, waiting for transfers between devices: none -> 180 us  [the longest x40 68.2 us: swap_dp(): return lax.ppermute(array, 'dp', [(i, i ^ bit) for i in range(dp)])]
    ppermute x0 -> x91, starting transfers between devices: none -> 172 us  [the longest x18 96.3 us: over_z(): lax.ppermute(ahead, 'dp', [(i, i + 4) for i in range(dp) if i // 4 < step])]
    dot_general x37 -> x0, matrix products: 162 us -> none  [the longest x9 33.4 us: plain_dot(): return jnp.dot(left_mat, right_mat, preferred_element_type=jnp.float32)]
    pallas_call x0 -> x20, Pallas kernels: none -> 118 us  [the longest x14 96.2 us: call(): pl.pallas_call(body, grid=grid, in_specs=[spec(a.shape, b, i) for a, b, i...]
    psum x1 -> x0, blocking collectives: 61.4 us -> none  [on_device(): lax.psum((grad_bquery, grad_bvalue, grad_bproj, grad_gain_attn, grad_shif...]
    unnamed x82 -> x160, local copies, waits for them, and re-layouts: 5.86 us -> 36 us
  transfers between devices with their start and end apart: 10 -> 91, of which waited for: 9 -> 28; matrix products, arithmetic and copies ran while one was open for 5% -> 7% of each run, Pallas kernels for 0% -> 19%
where the time goes in v1:
time: 553 us; the launch traced here: 547 us
  waiting for transfers between devices  180 us (33%)
  starting transfers between devices  172 us (31%)
  Pallas kernels  118 us (21%)
  local copies, waits for them, and re-layouts  46.8 us (8%)
  other arithmetic  28 us (5%)
    ppermute x18, starting transfers between devices, over_z(): lax.ppermute(ahead, 'dp', [(i, i + 4) for i in range(dp) if i // 4 < step])  96.3 us
    pallas_call x14, Pallas kernels, call(): pl.pallas_call(body, grid=grid, in_specs=[spec(a.shape, b, i) for a, b, i...  96.2 us
    ppermute x40, waiting for transfers between devices, swap_dp(): return lax.ppermute(array, 'dp', [(i, i ^ bit) for i in range(dp)])  68.2 us
    ppermute x15, waiting for transfers between devices, swap_mp(): return lax.ppermute(array, 'mp', [(0, 1), (1, 0)])  49.4 us
    ppermute x40, starting transfers between devices, swap_dp(): return lax.ppermute(array, 'dp', [(i, i ^ bit) for i in range(dp)])  40.8 us
    ppermute x18, waiting for transfers between devices, over_z(): lax.ppermute(ahead, 'dp', [(i, i + 4) for i in range(dp) if i // 4 < step])  38 us
    unnamed x160, local copies, waits for them, and re-layouts  36 us
    ppermute x18, waiting for transfers between devices, over_z(): lax.ppermute(behind, 'dp', [(i, i - 4) for i in range(dp) if i // 4 >= le...  24.2 us
  transfers between devices with their start and end apart: 91, of which 28 were waited for; matrix products, arithmetic and copies ran while one was open for 7% of the time, Pallas kernels for 19%

profile of v1, /device:TPU:0, one launch (start us, length us, event | category | flops | bytes accessed | tf_op | source)
XLA Modules:
  0.0 546.9 jit_solution(11257820212336625821)
XLA Ops:
  10.6 8.4 %collective-permute-done.13 = f32[96,1536]{1,0:T(8,128)S(1)} collective-permute-done((f32[96,1536]{1,0:T(8,128)S(1)}, f32[96,1536]{1,0:T(8,128)S(1)}, u32[]{:S(2)}, u32[]{:S(2)}) %collective-permute-start.13) | collective-permute-done | bytes 589856 | tf_op jit(solution)/shard_map/ppermute | solution.py:350
  21.1 7.4 %collective-permute-done = f32[96,1152]{1,0:T(8,128)S(1)} collective-permute-done((f32[96,1152]{1,0:T(8,128)}, f32[96,1152]{1,0:T(8,128)S(1)}, u32[]{:S(2)}, u32[]{:S(2)}) %collective-permute-start) | collective-permute-done | bytes 442400 | tf_op jit(solution)/shard_map/ppermute | solution.py:350
  32.6 7.8 %collective-permute-done.19 = f32[192,768]{1,0:T(8,128)S(1)} collective-permute-done((f32[192,768]{1,0:T(8,128)S(1)}, f32[192,768]{1,0:T(8,128)S(1)}, u32[]{:S(2)}, u32[]{:S(2)}) %collective-permute-start.19) | collective-permute-done | bytes 589856 | tf_op jit(solution)/shard_map/ppermute | solution.py:350
  45.9 10.4 %collective-permute-done.15 = f32[96,1536]{1,0:T(8,128)S(1)} collective-permute-done((f32[96,1536]{1,0:T(8,128)S(1)}, f32[96,1536]{1,0:T(8,128)S(1)}, u32[]{:S(2)}, u32[]{:S(2)}) %collective-permute-start.15) | collective-permute-done | bytes 589856 | tf_op jit(solution)/shard_map/ppermute | solution.py:353
  57.9 15.8 %collective-permute-done.4 = f32[48,1152]{1,0:T(8,128)S(1)} collective-permute-done((f32[48,1152]{1,0:T(8,128)S(1)}, f32[48,1152]{1,0:T(8,128)S(1)}, u32[]{:S(2)}, u32[]{:S(2)}) %collective-permute-start.4) | collective-permute-done | bytes 221216 | tf_op jit(solution)/shard_map/ppermute | solution.py:353
  113.2 9.3 %shard_map.314 = (bf16[512,384]{1,0:T(8,128)(2,1)S(1)}, bf16[512,384]{1,0:T(8,128)(2,1)S(1)}, bf16[512,384]{1,0:T(8,128)(2,1)S(1)}, bf16[512,384]{1,0:T(8,128)(2,1)S(1)}, f32[6,512]{1,0:T(8,128)S(1)}) custom-call(bf16[512,768]{1,0:T(8,128)(2,1)} %constant_dynamic-slice_fusion.4.x_ref.left_ref, bf16[768,384]{1,0:T(8,128)(2,1)S(1)} %copy-done.22, ...), custom_call_target="tpu_custom_call" | custom-call | flops 2516582400 | bytes 4150272 | tf_op jit(solution)/shard_map/pallas_call | solution.py:40
  134.5 9.4 %shard_map.316 = (bf16[512,384]{1,0:T(8,128)(2,1)S(1)}, bf16[512,384]{1,0:T(8,128)(2,1)S(1)}, bf16[512,384]{1,0:T(8,128)(2,1)S(1)}, bf16[512,384]{1,0:T(8,128)(2,1)S(1)}, f32[6,512]{1,0:T(8,128)S(1)}) custom-call(bf16[512,768]{1,0:T(8,128)(2,1)S(1)} %copy-done.19, bf16[768,1152]{1,0:T(8,128)(2,1)} %copy-done.2, bf16[768,1152]{1,0:T(8,128)(2,1)} %copy-done.2, ...), custom_call_target="tpu_custom_call" | custom-call | flops 2516582400 | bytes 7689216 | tf_op jit(solution)/shard_map/pallas_call | solution.py:40
  144.0 8.9 %shard_map.318 = (f32[512,768]{1,0:T(8,128)}, bf16[512,768]{1,0:T(8,128)(2,1)S(1)}, f32[512,768]{1,0:T(8,128)}, bf16[512,1536]{1,0:T(8,128)(2,1)}, f32[512,1536]{1,0:T(8,128)}) custom-call(bf16[512,768]{1,0:T(8,128)(2,1)S(1)} %copy-done.19, bf16[512,384]{1,0:T(8,128)(2,1)S(1)} %copy-done.49, bf16[512,384]{1,0:T(8,128)(2,1)S(1)} %get-tuple-element.63.cx_ref.oth_ref, ...), custom_call_target="tpu_custom_call" | custom-call | flops 3019898880 | bytes 16140288 | tf_op jit(solution)/shard_map/pallas_call | solution.py:40
  152.9 5.5 %shard_map.319.wu_ref.wux_ref = bf16[768,1536]{1,0:T(8,128)(2,1)S(1)} custom-call(s32[2]{0:T(128)S(1)} %pad_add_fusion.place_ref, f32[4,96,1536]{2,1,0:T(8,128)} %pad_maximum_fusion.mine_ref, f32[4,96,1536]{2,1,0:T(8,128)} %collective-permute-done.18.theirs_ref), custom_call_target="tpu_custom_call" | custom-call | bytes 7077888 | tf_op jit(solution)/shard_map/pallas_call | solution.py:376
  159.9 5.5 %shard_map.320.wd_ref.wdx_ref = bf16[1536,768]{1,0:T(8,128)(2,1)S(1)} custom-call(s32[2]{0:T(128)S(1)} %pad_add_fusion.place_ref, f32[4,192,768]{2,1,0:T(8,128)} %pad_maximum_fusion.1.mine_ref, f32[4,192,768]{2,1,0:T(8,128)} %collective-permute-done.24.theirs_ref), custom_call_target="tpu_custom_call" | custom-call | bytes 7077888 | tf_op jit(solution)/shard_map/pallas_call | solution.py:376
  166.8 9.8 %shard_map.321 = (bf16[512,1536]{1,0:T(8,128)(2,1)S(1)}, f32[512,1536]{1,0:T(8,128)}, f32[512,768]{1,0:T(8,128)}, f32[512,768]{1,0:T(8,128)}, bf16[512,768]{1,0:T(8,128)(2,1)S(1)}, /*index=5*/f32[8,768]{1,0:T(8,128)S(1)}) custom-call(bf16[512,768]{1,0:T(8,128)(2,1)S(1)} %get-tuple-element.64.nlow_ref.left_ref, f32[512,768]{1,0:T(8,128)} %get-tuple-element.65.start_ref, ...), custom_call_target="tpu_custom_call" | custom-call | flops 2415919104 | bytes 16551936 | tf_op jit(solution)/shard_map/pallas_call | solution.py:40
  179.4 15.1 %shard_map.323 = (bf16[512,1536]{1,0:T(8,128)(2,1)}, bf16[512,1536]{1,0:T(8,128)(2,1)}, f32[8,1536]{1,0:T(8,128)S(1)}, f32[512,768]{1,0:T(8,128)}, bf16[512,768]...) custom-call(bf16[512,768]{1,0:T(8,128)(2,1)S(1)} %get-tuple-element.67.dffn, ...), custom_call_target="tpu_custom_call" | custom-call | flops 4831838208 | bytes 27208704 | tf_op jit(solution)/shard_map/pallas_call | solution.py:40
  198.4 7.1 %shard_map.325 = (bf16[512,1152]{1,0:T(8,128)(2,1)S(1)}, f32[8,1152]{1,0:T(8,128)S(1)}) custom-call(bf16[512,384]{1,0:T(8,128)(2,1)S(1)} %get-tuple-element.79.q_ref, bf16[512,384]{1,0:T(8,128)(2,1)S(1)} %get-tuple-element.80.k_ref, bf16[512,384]{1,0:T(8,128)(2,1)S(1)} %get-tuple-element.81.v_ref, f32[6,512]{1,0:T(8,128)S(1)} %get-tuple-element.82.lse_ref, ...), custom_call_target="tpu_custom_call" | custom-call | flops 4026531840 | bytes 2807808 | tf_op jit(solution)/shard_map/pallas_call | solution.py:40
  211.8 7.1 %shard_map.324 = (bf16[512,1152]{1,0:T(8,128)(2,1)S(1)}, f32[8,1152]{1,0:T(8,128)S(1)}) custom-call(bf16[512,384]{1,0:T(8,128)(2,1)S(1)} %copy-done.51, bf16[512,384]{1,0:T(8,128)(2,1)S(1)} %copy-done.53, bf16[512,384]{1,0:T(8,128)(2,1)S(1)} %copy-done.55, f32[6,512]{1,0:T(8,128)S(1)} %get-tuple-element.76.lse_ref, bf16[512,384]{1,0:T(8,128)(2,1)S(1)} %copy-done.39, ...), custom_call_target="tpu_custom_call" | custom-call | flops 4026531840 | bytes 2807808 | tf_op jit(solution)/shard_map/pallas_call | solution.py:40
  236.1 5.8 %shard_map.326.mine_ref = f32[512,768]{1,0:T(8,128)} custom-call(f32[512,768]{1,0:T(8,128)} %get-tuple-element.72.refs_0_, bf16[512,1152]{1,0:T(8,128)(2,1)S(1)} %copy-done.12, bf16[512,1152]{1,0:T(8,128)(2,1)S(1)} %get-tuple-element.84.refs_2_.oth_ref, bf16[768,384]{1,0:T(8,128)(2,1)S(1)} %copy-done.23, bf16[768,384]{1,0:T(8,128)(2,1)S(1)} %copy-done.25, ...), custom_call_target="tpu_custom_call" | custom-call | flops 1811939328 | bytes 12582912 | tf_op jit(solution)/shard_map/pallas_call | solution.py:40
  307.2 6.9 %collective-permute-done.48 = f32[2,48,384]{2,1,0:T(8,128)S(1)} collective-permute-done((f32[2,48,384]{2,1,0:T(8,128)S(1)}, f32[2,48,384]{2,1,0:T(8,128)S(1)}, u32[]{:S(2)}, u32[]{:S(2)}) %collective-permute-start.48) | collective-permute-done | bytes 147488 | tf_op jit(solution)/shard_map/ppermute | solution.py:500
  326.0 16.8 %collective-permute-done.49 = f32[48,384]{1,0:T(8,128)S(1)} collective-permute-done((f32[48,384]{1,0:T(8,128)S(1)}, f32[48,384]{1,0:T(8,128)S(1)}, u32[]{:S(2)}, u32[]{:S(2)}) %collective-permute-start.49) | collective-permute-done | bytes 73760 | tf_op jit(solution)/shard_map/ppermute | solution.py:350
  351.7 20.3 %collective-permute-done.74 = f32[2,4,48,768]{3,2,1,0:T(8,128)S(1)} collective-permute-done((f32[2,4,48,768]{3,2,1,0:T(8,128)S(1)}, f32[2,4,48,768]{3,2,1,0:T(8,128)S(1)}, u32[]{:S(2)}, u32[]{:S(2)}) %collective-permute-start.74) | collective-permute-done | bytes 1179680 | tf_op jit(solution)/shard_map/ppermute | solution.py:353
  407.8 15.0 %collective-permute-done.67 = f32[48,768]{1,0:T(8,128)S(1)} collective-permute-done((f32[48,768]{1,0:T(8,128)S(1)}, f32[48,768]{1,0:T(8,128)S(1)}, u32[]{:S(2)}, u32[]{:S(2)}) %collective-permute-start.67) | collective-permute-done | bytes 147488 | tf_op jit(solution)/shard_map/ppermute | solution.py:497
  436.5 6.4 %collective-permute-start.29 = (f32[2,2,48,1152]{3,2,1,0:T(8,128)S(1)}, f32[2,2,48,1152]{3,2,1,0:T(8,128)S(1)}, u32[]{:S(2)}, u32[]{:S(2)}) collective-permute-start(f32[2,2,48,1152]{3,2,1,0:T(8,128)S(1)} %bitcast_add_fusion.4), channel_id=1, source_target_pairs={{0,8},{2,10},{4,12},{6,14},{8,16},{10,18},{12,20},{14,22},{1,9},{3... | collective-permute-start | bytes 2654216 | tf_op jit(solution)/shard_map/ppermute | solution.py:497
  450.3 14.0 %collective-permute-done.59 = f32[48,768]{1,0:T(8,128)S(1)} collective-permute-done((f32[48,768]{1,0:T(8,128)S(1)}, f32[48,768]{1,0:T(8,128)S(1)}, u32[]{:S(2)}, u32[]{:S(2)}) %collective-permute-start.59) | collective-permute-done | bytes 147488 | tf_op jit(solution)/shard_map/ppermute | solution.py:497
  469.3 28.3 %collective-permute-start.69 = (f32[48,768]{1,0:T(8,128)S(1)}, f32[48,768]{1,0:T(8,128)S(1)}, u32[]{:S(2)}, u32[]{:S(2)}) collective-permute-start(f32[48,768]{1,0:T(8,128)S(1)} %get-tuple-element.133), channel_id=1, source_target_pairs={{0,8},{2,10},{4,12},{6,14},{8,16},{10,18},{12,20},{14,22},{16,24},... | collective-permute-start | bytes 442376 | tf_op jit(solution)/shard_map/ppermute | solution.py:497
  513.2 17.3 %collective-permute-done.63 = f32[48,768]{1,0:T(8,128)S(1)} collective-permute-done((f32[48,768]{1,0:T(8,128)S(1)}, f32[48,768]{1,0:T(8,128)S(1)}, u32[]{:S(2)}, u32[]{:S(2)}) %collective-permute-start.63) | collective-permute-done | bytes 147488 | tf_op jit(solution)/shard_map/ppermute | solution.py:500
  533.6 6.3 %collective-permute-done.34 = f32[2,48,1152]{2,1,0:T(8,128)S(1)} collective-permute-done((f32[2,48,1152]{2,1,0:T(8,128)S(1)}, f32[2,48,1152]{2,1,0:T(8,128)S(1)}, u32[]{:S(2)}, u32[]{:S(2)}) %collective-permute-start.34) | collective-permute-done | bytes 442400 | tf_op jit(solution)/shard_map/ppermute | solution.py:353
  (466 shorter events, 279.6 us)
Async XLA Ops:
  40.3 33.5 %collective-permute-start.20 = (f32[192,768]{1,0:T(8,128)S(1)}, f32[192,768]{1,0:T(8,128)S(1)}, u32[]{:S(2)}, u32[]{:S(2)}) collective-permute-start(f32[192,768]{1,0:T(8,128)S(1)} %collective-permute-done.19), channel_id=1, source_target_pairs={{0,4},{2,6},{4,0},{6,2},{8,12},{10,14},{12,8},{14,10},{16,20},{18,... | collective-permute-start | bytes 1769480 | tf_op jit(solution)/shard_map/ppermute | solution.py:353
  42.2 33.7 %collective-permute-start.21 = (f32[192,768]{1,0:T(8,128)S(1)}, f32[192,768]{1,0:T(8,128)S(1)}, u32[]{:S(2)}, u32[]{:S(2)}) collective-permute-start(f32[192,768]{1,0:T(8,128)S(1)} %collective-permute-done.19), channel_id=1, source_target_pairs={{0,8},{2,10},{4,12},{6,14},{8,0},{10,2},{12,4},{14,6},{16,24},{18,... | collective-permute-start | bytes 1769480 | tf_op jit(solution)/shard_map/ppermute | solution.py:353
  82.1 70.8 %collective-permute-start.18 = (f32[4,96,1536]{2,1,0:T(8,128)}, f32[4,96,1536]{2,1,0:T(8,128)}, u32[]{:S(2)}, u32[]{:S(2)}) collective-permute-start(f32[4,96,1536]{2,1,0:T(8,128)} %pad_maximum_fusion.mine_ref), channel_id=1, source_target_pairs={{0,2},{2,0},{4,6},{6,4},{8,10},{10,8},{12,14},{14,12},{16,18},{18,... | collective-permute-start | bytes 7077896 | tf_op jit(solution)/shard_map/ppermute | solution.py:353
  85.2 74.7 %collective-permute-start.24 = (f32[4,192,768]{2,1,0:T(8,128)}, f32[4,192,768]{2,1,0:T(8,128)}, u32[]{:S(2)}, u32[]{:S(2)}) collective-permute-start(f32[4,192,768]{2,1,0:T(8,128)} %pad_maximum_fusion.1.mine_ref), channel_id=1, source_target_pairs={{0,2},{2,0},{4,6},{6,4},{8,10},{10,8},{12,14},{14,12},{16,18},{18,... | collective-permute-start | bytes 7077896 | tf_op jit(solution)/shard_map/ppermute | solution.py:353
  85.4 43.9 %collective-permute-start.5 = (f32[4,96,1152]{2,1,0:T(8,128)S(1)}, f32[4,96,1152]{2,1,0:T(8,128)}, u32[]{:S(2)}, u32[]{:S(2)}) collective-permute-start(f32[4,96,1152]{2,1,0:T(8,128)S(1)} %pad_maximum_fusion.2.mine_ref), channel_id=1, source_target_pairs={{0,2},{2,0},{4,6},{6,4},{8,10},{10,8},{12,14},{14,12},{16,18},{18,... | collective-permute-start | bytes 5308424 | tf_op jit(solution)/shard_map/ppermute | solution.py:353
  177.9 86.4 %collective-permute-start.25 = (f32[512,768]{1,0:T(8,128)}, f32[512,768]{1,0:T(8,128)S(1)}, u32[]{:S(2)}, u32[]{:S(2)}) collective-permute-start(f32[512,768]{1,0:T(8,128)} %get-tuple-element.66.mine_ref), channel_id=1, source_target_pairs={{0,1},{1,0},{2,3},{3,2},{4,5},{5,4},{6,7},{7,6},{8,9},{9,8},{10,11... | collective-permute-start | bytes 4718600 | tf_op jit(solution)/shard_map/ppermute | solution.py:350
  224.3 73.3 %collective-permute-start.64 = (f32[2,4,2,48,768]{4,3,2,1,0:T(8,128)}, f32[2,4,2,48,768]{4,3,2,1,0:T(8,128)}, u32[]{:S(2)}, u32[]{:S(2)}) collective-permute-start(f32[2,4,2,48,768]{4,3,2,1,0:T(8,128)} %get-tuple-element.100), channel_id=1, source_target_pairs={{0,2},{2,0},{4,6},{6,4},{8,10},{10,8},{12,14},{14,12},{16,18},{18,... | collective-permute-start | bytes 7077896 | tf_op jit(solution)/shard_map/ppermute | solution.py:353
  244.1 36.0 %collective-permute-start.26 = (f32[512,768]{1,0:T(8,128)}, f32[512,768]{1,0:T(8,128)S(1)}, u32[]{:S(2)}, u32[]{:S(2)}) collective-permute-start(f32[512,768]{1,0:T(8,128)} %shard_map.326.mine_ref), channel_id=1, source_target_pairs={{0,1},{1,0},{2,3},{3,2},{4,5},{5,4},{6,7},{7,6},{8,9},{9,8},{10,11... | collective-permute-start | bytes 4718600 | tf_op jit(solution)/shard_map/ppermute | solution.py:350
  261.9 53.7 %collective-permute-start.82 = (f32[2,4,2,48,768]{4,3,2,1,0:T(8,128)}, f32[2,4,2,48,768]{4,3,2,1,0:T(8,128)}, u32[]{:S(2)}, u32[]{:S(2)}) collective-permute-start(f32[2,4,2,48,768]{4,3,2,1,0:T(8,128)} %get-tuple-element.106), channel_id=1, source_target_pairs={{0,2},{2,0},{4,6},{6,4},{8,10},{10,8},{12,14},{14,12},{16,18},{18,... | collective-permute-start | bytes 7077896 | tf_op jit(solution)/shard_map/ppermute | solution.py:353
  274.5 45.2 %collective-permute-start.73 = (f32[2,4,2,48,768]{4,3,2,1,0:T(8,128)}, f32[2,4,2,48,768]{4,3,2,1,0:T(8,128)}, u32[]{:S(2)}, u32[]{:S(2)}) collective-permute-start(f32[2,4,2,48,768]{4,3,2,1,0:T(8,128)} %get-tuple-element.104), channel_id=1, source_target_pairs={{0,2},{2,0},{4,6},{6,4},{8,10},{10,8},{12,14},{14,12},{16,18},{18,... | collective-permute-start | bytes 7077896 | tf_op jit(solution)/shard_map/ppermute | solution.py:353
  278.7 43.7 %collective-permute-start.55 = (f32[2,4,2,48,768]{4,3,2,1,0:T(8,128)}, f32[2,4,2,48,768]{4,3,2,1,0:T(8,128)}, u32[]{:S(2)}, u32[]{:S(2)}) collective-permute-start(f32[2,4,2,48,768]{4,3,2,1,0:T(8,128)} %get-tuple-element.98), channel_id=1, source_target_pairs={{0,2},{2,0},{4,6},{6,4},{8,10},{10,8},{12,14},{14,12},{16,18},{18,... | collective-permute-start | bytes 7077896 | tf_op jit(solution)/shard_map/ppermute | solution.py:353
  291.2 86.5 %collective-permute-start.27 = (f32[2,4,2,48,1152]{4,3,2,1,0:T(8,128)}, f32[2,4,2,48,1152]{4,3,2,1,0:T(8,128)}, u32[]{:S(2)}, u32[]{:S(2)}) collective-permute-start(f32[2,4,2,48,1152]{4,3,2,1,0:T(8,128)} %get-tuple-element.86), channel_id=1, source_target_pairs={{0,2},{2,0},{4,6},{6,4},{8,10},{10,8},{12,14},{14,12},{16,18},{18,... | collective-permute-start | bytes 10616840 | tf_op jit(solution)/shard_map/ppermute | solution.py:353
  322.3 49.6 %collective-permute-start.74 = (f32[2,4,48,768]{3,2,1,0:T(8,128)S(1)}, f32[2,4,48,768]{3,2,1,0:T(8,128)S(1)}, u32[]{:S(2)}, u32[]{:S(2)}) collective-permute-start(f32[2,4,48,768]{3,2,1,0:T(8,128)S(1)} %dynamic-slice_bitcast_fusion.1), channel_id=1, source_target_pairs={{0,4},{2,6},{4,0},{6,2},{8,12},{10,14},{12,8},{14,10},{16,20},{18,... | collective-permute-start | bytes 3538952 | tf_op jit(solution)/shard_map/ppermute | solution.py:353
  345.1 52.9 %collective-permute-start.66 = (f32[4,48,768]{2,1,0:T(8,128)S(1)}, f32[4,48,768]{2,1,0:T(8,128)S(1)}, u32[]{:S(2)}, u32[]{:S(2)}) collective-permute-start(f32[4,48,768]{2,1,0:T(8,128)S(1)} %dynamic-slice_bitcast_fusion.4), channel_id=1, source_target_pairs={{0,4},{2,6},{4,0},{6,2},{8,12},{10,14},{12,8},{14,10},{16,20},{18,... | collective-permute-start | bytes 1769480 | tf_op jit(solution)/shard_map/ppermute | solution.py:353
  347.3 33.9 %collective-permute-start.84 = (f32[2,48,768]{2,1,0:T(8,128)S(1)}, f32[2,48,768]{2,1,0:T(8,128)S(1)}, u32[]{:S(2)}, u32[]{:S(2)}) collective-permute-start(f32[2,48,768]{2,1,0:T(8,128)S(1)} %get-tuple-element.127), channel_id=1, source_target_pairs={{0,8},{2,10},{4,12},{6,14},{1,9},{3,11},{5,13},{7,15}} | collective-permute-start | bytes 884744 | tf_op jit(solution)/shard_map/ppermute | solution.py:497
  389.1 42.2 %collective-permute-start.28 = (f32[2,2,48,1152]{3,2,1,0:T(8,128)S(1)}, f32[2,2,48,1152]{3,2,1,0:T(8,128)S(1)}, u32[]{:S(2)}, u32[]{:S(2)}) collective-permute-start(f32[2,2,48,1152]{3,2,1,0:T(8,128)S(1)} %get-tuple-element.119), channel_id=1, source_target_pairs={{0,8},{2,10},{4,12},{6,14},{1,9},{3,11},{5,13},{7,15}} | collective-permute-start | bytes 2654216 | tf_op jit(solution)/shard_map/ppermute | solution.py:497
  391.1 75.2 %collective-permute-start.31 = (f32[2,2,48,1152]{3,2,1,0:T(8,128)S(1)}, f32[2,2,48,1152]{3,2,1,0:T(8,128)S(1)}, u32[]{:S(2)}, u32[]{:S(2)}) collective-permute-start(f32[2,2,48,1152]{3,2,1,0:T(8,128)S(1)} %get-tuple-element.120), channel_id=1, source_target_pairs={{24,16},{26,18},{28,20},{30,22},{25,17},{27,19},{29,21},{31,23}} | collective-permute-start | bytes 2654216 | tf_op jit(solution)/shard_map/ppermute | solution.py:500
  397.2 33.4 %collective-permute-start.88 = (f32[2,48,768]{2,1,0:T(8,128)S(1)}, f32[2,48,768]{2,1,0:T(8,128)S(1)}, u32[]{:S(2)}, u32[]{:S(2)}) collective-permute-start(f32[2,48,768]{2,1,0:T(8,128)S(1)} %get-tuple-element.126), channel_id=1, source_target_pairs={{16,8},{18,10},{20,12},{22,14},{24,16},{26,18},{28,20},{30,22},{17... | collective-permute-start | bytes 884744 | tf_op jit(solution)/shard_map/ppermute | solution.py:500
  398.0 71.3 %collective-permute-start.86 = (f32[2,48,768]{2,1,0:T(8,128)S(1)}, f32[2,48,768]{2,1,0:T(8,128)S(1)}, u32[]{:S(2)}, u32[]{:S(2)}) collective-permute-start(f32[2,48,768]{2,1,0:T(8,128)S(1)} %get-tuple-element.125), channel_id=1, source_target_pairs={{0,8},{2,10},{4,12},{6,14},{8,16},{10,18},{12,20},{14,22},{16,24},... | collective-permute-start | bytes 884744 | tf_op jit(solution)/shard_map/ppermute | solution.py:497
  445.9 56.4 %collective-permute-start.77 = (f32[2,48,768]{2,1,0:T(8,128)S(1)}, f32[2,48,768]{2,1,0:T(8,128)S(1)}, u32[]{:S(2)}, u32[]{:S(2)}) collective-permute-start(f32[2,48,768]{2,1,0:T(8,128)S(1)} %get-tuple-element.121), channel_id=1, source_target_pairs={{0,8},{2,10},{4,12},{6,14},{8,16},{10,18},{12,20},{14,22},{16,24},... | collective-permute-start | bytes 884744 | tf_op jit(solution)/shard_map/ppermute | solution.py:497
  465.0 32.6 %collective-permute-start.89 = (f32[2,48,768]{2,1,0:T(8,128)S(1)}, f32[2,48,768]{2,1,0:T(8,128)S(1)}, u32[]{:S(2)}, u32[]{:S(2)}) collective-permute-start(f32[2,48,768]{2,1,0:T(8,128)S(1)} %bitcast_add_fusion.12), channel_id=1, source_target_pairs={{8,0},{10,2},{12,4},{14,6},{16,8},{18,10},{20,12},{22,14},{24,16},... | collective-permute-start | bytes 884744 | tf_op jit(solution)/shard_map/ppermute | solution.py:500
  466.3 37.2 %collective-permute-start.80 = (f32[2,48,768]{2,1,0:T(8,128)S(1)}, f32[2,48,768]{2,1,0:T(8,128)S(1)}, u32[]{:S(2)}, u32[]{:S(2)}) collective-permute-start(f32[2,48,768]{2,1,0:T(8,128)S(1)} %bitcast_add_fusion.17), channel_id=1, source_target_pairs={{8,0},{10,2},{12,4},{14,6},{16,8},{18,10},{20,12},{22,14},{24,16},... | collective-permute-start | bytes 884744 | tf_op jit(solution)/shard_map/ppermute | solution.py:500
  468.6 39.7 %collective-permute-start.32 = (f32[2,2,48,1152]{3,2,1,0:T(8,128)S(1)}, f32[2,2,48,1152]{3,2,1,0:T(8,128)S(1)}, u32[]{:S(2)}, u32[]{:S(2)}) collective-permute-start(f32[2,2,48,1152]{3,2,1,0:T(8,128)S(1)} %get-tuple-element.118), channel_id=1, source_target_pairs={{16,8},{18,10},{20,12},{22,14},{24,16},{26,18},{28,20},{30,22},{17... | collective-permute-start | bytes 2654216 | tf_op jit(solution)/shard_map/ppermute | solution.py:500
  469.3 40.3 %collective-permute-start.69 = (f32[48,768]{1,0:T(8,128)S(1)}, f32[48,768]{1,0:T(8,128)S(1)}, u32[]{:S(2)}, u32[]{:S(2)}) collective-permute-start(f32[48,768]{1,0:T(8,128)S(1)} %get-tuple-element.133), channel_id=1, source_target_pairs={{0,8},{2,10},{4,12},{6,14},{8,16},{10,18},{12,20},{14,22},{16,24},... | collective-permute-start | bytes 442376 | tf_op jit(solution)/shard_map/ppermute | solution.py:497
  (147 other events, 1591.1 us)
